TPU v7x, 32 devices: a whole 2x2x4 slice. The times are simulated.
32 devices in a mesh: pos: 8 (over z, x), exp: 4 (over y, core).
Axes of the slice: x: 2, y: 2, z: 4, core: 2. Of those that a mesh axis runs over, the one named last changes fastest.
Arguments:
- patches: bfloat16 [8192, 4, 256], P(('pos', 'exp')), may hold values from -6 to 6
- conv_weight: bfloat16 [3, 256, 2048], replicated, may hold values from -0.21875 to 0.21875
- phi: bfloat16 [2048, 32], replicated, may hold values from -40 to 40, as said below
- w_in: bfloat16 [4, 2048, 8192], P('exp', None, 'pos'), may hold values from -0.125 to 0.125
- w_out: bfloat16 [4, 8192, 2048], P('exp', 'pos'), may hold values from -0.0625 to 0.0625
Outputs:
- mixed: bfloat16 [8192, 4, 2048], P(('pos', 'exp'))
Inputs may be any that keep to these rules, and one draw needn't show every extreme that they name: phi is real-valued.
All inputs are finite; a program needn't handle non-finite values.
Results may differ from a plain program's by a relative error of at most 0.019.
The roundings to bfloat16 on the way count: a program that leaves them out, or rounds other values in their place, can miss the bound.
Values may be sent and summed in bfloat16 or wider, within the bound.
A program may use at most 128 MiB of HBM per device.

v0:
```python
import jax
import jax.numpy as jnp
from jax import lax
from jax.sharding import PartitionSpec as P

D = 2048
SLOTS_PER = 8


def with_halo(array, sides, width):
    for axis, dim in sides:
        count, length = (lax.axis_size(axis), array.shape[dim])
        up = [(i, (i + 1) % count) for i in range(count - 1)]
        down = [(j, i) for i, j in up]
        last = lax.slice_in_dim(array, length - width, length, axis=dim)
        initial = lax.slice_in_dim(array, 0, width, axis=dim)
        before = lax.ppermute(last, axis, up)
        after = lax.ppermute(initial, axis, down)
        array = jnp.concatenate([before, array, after], axis=dim)
    return array


def per_device(patches, conv_weight, phi, w_in, w_out):
    channels, periods, samples = patches.shape
    padded = with_halo(patches, ((("pos", "exp"), 0),), 1)
    running = jnp.zeros((channels * periods, D), jnp.float32)
    for offset in range(3):
        window = padded[offset : offset + channels].reshape(channels * periods, samples)
        running = running + jnp.dot(window, conv_weight[offset], preferred_element_type=jnp.float32)
    flat = running.astype(jnp.bfloat16)
    logits = jnp.dot(flat, phi, preferred_element_type=jnp.float32)
    local_peak = jnp.max(logits, axis=0)
    column_peak = lax.pmax(local_peak, ("pos", "exp"))
    raw_weights = jnp.exp(logits - column_peak)
    column_total = lax.psum(jnp.sum(raw_weights, axis=0), ("pos", "exp"))
    dispatch = (raw_weights / column_total).astype(jnp.bfloat16)
    group = lax.axis_index("exp")
    every_slot = lax.dot_general(
        dispatch, flat, (((0,), (0,)), ((), ())), preferred_element_type=jnp.float32
    )
    summed = lax.psum(every_slot, ("pos", "exp"))
    owned = lax.dynamic_slice_in_dim(summed, group * SLOTS_PER, SLOTS_PER, 0)
    slot_in = owned.astype(jnp.bfloat16)
    hidden = jax.nn.gelu(
        jnp.dot(slot_in, w_in[0], preferred_element_type=jnp.float32), approximate=True
    ).astype(jnp.bfloat16)
    expert_term = jnp.dot(hidden, w_out[0], preferred_element_type=jnp.float32)
    slot_out = lax.psum(expert_term, "pos").astype(jnp.bfloat16)
    row_peak = jnp.max(logits, axis=1, keepdims=True)
    row_weights = jnp.exp(logits - row_peak)
    combine = (row_weights / jnp.sum(row_weights, axis=1, keepdims=True)).astype(jnp.bfloat16)
    mixed = jnp.dot(
        combine,
        lax.all_gather(slot_out, "exp", axis=0, tiled=True),
        preferred_element_type=jnp.float32,
    )
    return mixed.astype(jnp.bfloat16).reshape(channels, periods, D)


def solution(mesh):
    in_specs = (
        P(("pos", "exp"), None, None),
        P(),
        P(),
        P("exp", None, "pos"),
        P("exp", "pos", None),
    )
    out_specs = P(("pos", "exp"), None, None)
    return jax.shard_map(
        per_device, mesh=mesh, in_specs=in_specs, out_specs=out_specs, check_vma=False
    )
```

profile of v0, /device:TPU:0, one launch (start us, length us, event | category | flops | bytes accessed | tf_op | source)
XLA Modules:
  0.0 222.8 jit_solution(4864337934841201705)
XLA Ops:
  0.0 0.0 copy-start
  0.0 0.7 fusion.47
  0.7 2.3 %collective-permute-start = (bf16[1,4,256]{2,1,0:T(4,128)(2,1)S(1)}, bf16[1,4,256]{2,1,0:T(4,128)(2,1)S(1)}, u32[]{:S(2)}, u32[]{:S(2)}) collective-permute-start(bf16[1,4,256]{2,1,0:T(4,128)(2,1)S(1)} %get-tuple-element.12), channel_id=1, source_target_pairs={{0,1},{1,2},{2,3},{3,4},{4,5},{5,6},{6,7},{7,8},{8,9},{9,10},{10,1... | collective-permute-start | bytes 6152 | tf_op jit(solution)/shard_map/ppermute | solution.py:17
  3.1 1.3 collective-permute-start.1
  4.4 2.0 reshape.17
  6.4 0.0 copy-start.2
  6.4 6.0 %fusion.8 = f32[1024,2048]{1,0:T(8,128)} fusion(bf16[1024,256]{1,0:T(8,128)(2,1)} %reshape.17, bf16[3,256,2048]{2,1,0:T(8,128)(2,1)} %param.6), kind=kOutput, calls=%fused_computation.8 | convolution fusion | flops 1073741824 | bytes 9961472 | tf_op jit(solution)/shard_map/dot_general | solution.py:29
  12.4 0.0 collective-permute-done
  12.4 0.0 collective-permute-done.1
  12.4 2.9 %pad_maximum_fusion = (bf16[256,4,256]{2,1,0:T(4,128)(2,1)}, bf16[256,4,256]{2,1,0:T(4,128)(2,1)}) fusion(bf16[1,4,256]{2,1,0:T(4,128)(2,1)S(1)} %collective-permute-done.1, bf16[256,4,256]{2,1,0:T(4,128)(2,1)} %param.5, bf16[1,4,256]{2,1,0:T(4,128)(2,1)S(1)} %collective-permute-done), kind=kLoop, calls=%fused_computation.15 | loop fusion | flops 524288 | bytes 1576960 | tf_op jit(solution)/shard_map/concatenate | solution.py:19
  15.3 2.0 reshape.16
  17.2 0.0 copy-done.2
  17.2 5.5 %fusion.10 = f32[1024,2048]{1,0:T(8,128)} fusion(bf16[1024,256]{1,0:T(8,128)(2,1)} %reshape.16, bf16[3,256,2048]{2,1,0:T(8,128)(2,1)S(1)} %copy-done.2), kind=kOutput, calls=%fused_computation.10 | convolution fusion | flops 1073741824 | bytes 9961472 | tf_op jit(solution)/shard_map/dot_general | solution.py:29
  22.7 2.0 reshape.18
  24.7 7.2 %add_convert_fusion = bf16[1024,2048]{1,0:T(8,128)(2,1)S(1)} fusion(f32[1024,2048]{1,0:T(8,128)} %fusion.10, f32[1024,2048]{1,0:T(8,128)} %fusion.8, bf16[1024,256]{1,0:T(8,128)(2,1)} %reshape.18, bf16[3,256,2048]{2,1,0:T(8,128)(2,1)S(1)} %copy-done.2), kind=kOutput, calls=%fused_computation | convolution fusion | flops 1080033280 | bytes 22544384 | tf_op jit(solution)/shard_map/dot_general | solution.py:29
  31.9 0.0 copy-start.1
  31.9 2.0 copy-done.1
  33.9 0.0 copy-done
  33.9 1.4 fusion.46
  35.3 44.7 %pmax.7 = f32[32]{0:T(128)S(1)} all-reduce(f32[32]{0:T(128)S(1)} %get-tuple-element.8), channel_id=1, replica_groups=mesh['pos'=8,'exp'=4] {'pos','exp'}, use_global_device_ids=true, to_apply=%region_3.0 | all-reduce | flops 32 | bytes 256 | tf_op jit(solution)/shard_map/pmax | solution.py:33
  80.0 0.2 fusion.15
  80.2 40.3 %psum.21 = f32[32]{0:T(128)S(1)} all-reduce(f32[32]{0:T(128)S(1)} %get-tuple-element.6), channel_id=1, replica_groups=mesh['pos'=8,'exp'=4] {'pos','exp'}, use_global_device_ids=true, to_apply=%region_5.0 | all-reduce | flops 32 | bytes 256 | tf_op jit(solution)/shard_map/psum | solution.py:35
  120.5 3.1 %fusion.17 = f32[32,2048]{1,0:T(8,128)S(1)} fusion(bf16[1024,2048]{1,0:T(8,128)(2,1)} %copy-done.1, f32[1024,32]{0,1:T(8,128)S(1)} %get-tuple-element.13, f32[32]{0:T(128)S(1)} %psum.21, f32[32]{0:T(128)S(1)} %pmax.7), kind=kOutput, calls=%fused_computation.23 | convolution fusion | flops 134316032 | bytes 4587776 | tf_op jit(solution)/shard_map/dot_general | solution.py:38
  123.6 42.5 %all-reduce.1 = bf16[32,2048]{1,0:T(8,128)(2,1)S(1)} all-reduce(f32[32,2048]{1,0:T(8,128)S(1)} %fusion.17), channel_id=1, replica_groups=mesh['pos'=8,'exp'=4] {'pos','exp'}, use_global_device_ids=true, to_apply=%region_6.0 | all-reduce | flops 65536 | bytes 393216 | tf_op jit(solution)/shard_map/psum | solution.py:41
  166.1 4.7 %fusion = f32[8,2048]{1,0:T(8,128)S(1)} fusion(bf16[1,1024,2048]{2,1,0:T(8,128)(2,1)} %param.9, bf16[1,2048,1024]{2,1,0:T(8,128)(2,1)} %param.8, bf16[32,2048]{1,0:T(8,128)(2,1)S(1)} %all-reduce.1, s32[]{:T(128)S(6)} %select_n.3), kind=kOutput, calls=%fused_computation.1 | convolution fusion | flops 67182592 | bytes 8486916 | tf_op jit(solution)/shard_map/dot_general | solution.py:47
  170.8 36.2 %psum.23 = bf16[8,2048]{1,0:T(8,128)(2,1)S(1)} all-reduce(f32[8,2048]{1,0:T(8,128)S(1)} %fusion), channel_id=1, replica_groups=mesh['pos'=8,'exp'=4] {'pos'}, use_global_device_ids=true, to_apply=%region_7.0 | all-reduce | flops 16384 | bytes 98304 | tf_op jit(solution)/shard_map/psum | solution.py:48
  207.0 5.4 %all_gather.3 = bf16[32,2048]{1,0:T(8,128)(2,1)S(1)} all-gather(bf16[8,2048]{1,0:T(8,128)(2,1)S(1)} %psum.23), channel_id=1, replica_groups=mesh['pos'=8,'exp'=4] {'exp'}, dimensions={0}, use_global_device_ids=true | all-gather | bytes 163840 | tf_op jit(solution)/shard_map/all_gather | solution.py:54
  212.5 3.2 %convolution_convert_fusion = bf16[1024,2048]{1,0:T(8,128)(2,1)} fusion(bf16[32,2048]{1,0:T(8,128)(2,1)S(1)} %all_gather.3, f32[1024,32]{0,1:T(8,128)S(1)} %get-tuple-element.13, f32[1024]{0:T(1024)S(1)} %get-tuple-element.5, f32[1024]{0:T(1024)S(1)} %get-tuple-element.7), kind=kOutput, calls=%fused_computation.5 | convolution fusion | flops 136413184 | bytes 4464640 | tf_op jit(solution)/shard_map/dot_general | solution.py:52
  215.7 7.2 %reshape.19 = bf16[256,4,2048]{2,1,0:T(4,128)(2,1)} reshape(bf16[1024,2048]{1,0:T(8,128)(2,1)} %convolution_convert_fusion) | data formatting | bytes 8388608 | tf_op jit(solution)/shard_map/reshape | solution.py:57
Async XLA Ops:
  0.0 33.9 %copy-start = (bf16[2048,32]{0,1:T(8,128)(2,1)S(1)}, bf16[2048,32]{0,1:T(8,128)(2,1)}, u32[]{:S(2)}) copy-start(bf16[2048,32]{0,1:T(8,128)(2,1)} %param.7) | copy-start | bytes 393220
  0.7 11.6 %collective-permute-start = (bf16[1,4,256]{2,1,0:T(4,128)(2,1)S(1)}, bf16[1,4,256]{2,1,0:T(4,128)(2,1)S(1)}, u32[]{:S(2)}, u32[]{:S(2)}) collective-permute-start(bf16[1,4,256]{2,1,0:T(4,128)(2,1)S(1)} %get-tuple-element.12), channel_id=1, source_target_pairs={{0,1},{1,2},{2,3},{3,4},{4,5},{5,6},{6,7},{7,8},{8,9},{9,10},{10,1... | collective-permute-start | bytes 6152 | tf_op jit(solution)/shard_map/ppermute | solution.py:17
  3.1 9.3 %collective-permute-start.1 = (bf16[1,4,256]{2,1,0:T(4,128)(2,1)S(1)}, bf16[1,4,256]{2,1,0:T(4,128)(2,1)S(1)}, u32[]{:S(2)}, u32[]{:S(2)}) collective-permute-start(bf16[1,4,256]{2,1,0:T(4,128)(2,1)S(1)} %get-tuple-element.11), channel_id=1, source_target_pairs={{1,0},{2,1},{3,2},{4,3},{5,4},{6,5},{7,6},{8,7},{9,8},{10,9},{11,1... | collective-permute-start | bytes 6152 | tf_op jit(solution)/shard_map/ppermute | solution.py:18
  6.4 10.9 %copy-start.2 = (bf16[3,256,2048]{2,1,0:T(8,128)(2,1)S(1)}, bf16[3,256,2048]{2,1,0:T(8,128)(2,1)}, u32[]{:S(2)}) copy-start(bf16[3,256,2048]{2,1,0:T(8,128)(2,1)} %param.6) | copy-start | bytes 9437188
  31.9 2.0 copy-start.1
where the time goes:
time: 224 us; the launch traced here: 223 us
  blocking collectives  169 us (75%)
  matrix products  31.1 us (14%)
  local copies, waits for them, and re-layouts  15.8 us (7%)
  starting transfers between devices  3.64 us (2%)
  other arithmetic  3.09 us (1%)
    pmax x1, blocking collectives, per_device(): column_peak = lax.pmax(local_peak, ('pos', 'exp'))  44.7 us
    psum x1, blocking collectives, per_device(): summed = lax.psum(every_slot, ('pos', 'exp'))  42.5 us
    psum x1, blocking collectives, per_device(): column_total = lax.psum(jnp.sum(raw_weights, axis=0), ('pos', 'exp'))  40.3 us
    psum x1, blocking collectives, per_device(): slot_out = lax.psum(expert_term, 'pos').astype(jnp.bfloat16)  36.2 us
    dot_general x3, matrix products, per_device(): jnp.dot(window, conv_weight[offset], preferred_element_type=jnp.float32)  18.7 us
    reshape x1, local copies, waits for them, and re-layouts, per_device(): return mixed.astype(jnp.bfloat16).reshape(channels, periods, D)  7.16 us
    reshape x3, local copies, waits for them, and re-layouts, per_device(): padded[offset:offset + channels].reshape(channels * periods, samples)  5.87 us
    all_gather x1, blocking collectives, per_device(): lax.all_gather(slot_out, 'exp', axis=0, tiled=True)  5.42 us
  transfers between devices with their start and end apart: 2, of which 0 were waited for; matrix products, arithmetic and copies ran while one was open for 4% of the time, Pallas kernels for 0%

commit v1 on v0

v1 whole, which is shorter than its diff:
```python
import functools

import jax
import jax.numpy as jnp
from jax import lax
from jax.experimental import pallas as pl
from jax.experimental.pallas import tpu as pltpu
from jax.sharding import PartitionSpec as P

MESH = pl.DeviceIdType.MESH
F32 = jnp.float32
BF16 = jnp.bfloat16


def pack(block):
    rows, width = block.shape
    if width % 256 == 0:
        half = width // 2
        return jnp.concatenate([block[:, :half], block[:, half:]], axis=0).astype(BF16)
    return jnp.concatenate([block, jnp.zeros_like(block)], axis=0).astype(BF16)


def packed_shape(rows, width):
    return (2 * rows, width // 2 if width % 256 == 0 else width)


def unpack(block, width):
    wide = block.astype(F32)
    rows = wide.shape[0] // 2
    if width % 256 == 0:
        return jnp.concatenate([wide[:rows], wide[rows:]], axis=1)
    return wide[:rows]


def layer_kernel(
    n_pos, n_exp, chunk,
    patches, taps, phi_t, w_in, w_out,
    combine_ref, slots_ref,
    x_raw, xs, taps_v, phi_v, win_v, wout_v, tokens, logits,
    halo_out, halo_in,
    stat_own, stat_exp, stat_mid, stat_pos,
    sum_own, sum_out, sum_exp,
    part_own, part_out, part_pos,
    in_own, in_all,
    term_own, term_out, term_pos,
    out_all,
    local_sem, chunk_sem,
    halo_s, halo_r, stat_es, stat_er, stat_ps, stat_pr,
    sum_s, sum_r, part_s, part_r, in_s, in_r, term_s, term_r,
    slot_s, slot_r, far_s, far_r,
):
    p, e = lax.axis_index("pos"), lax.axis_index("exp")
    count = n_pos * n_exp
    g = p * n_exp + e
    channels, periods, samples = x_raw.shape
    rows = channels * periods
    d = tokens.shape[1]
    n_slots = phi_v.shape[0]
    per = n_slots // n_exp
    blk = d // n_pos
    n_chunks = d // chunk
    edge = rows // 4

    right, left = lax.rem(g + 1, count), lax.rem(g + count - 1, count)
    right_id = (right // n_exp, lax.rem(right, n_exp))
    left_id = (left // n_exp, lax.rem(left, n_exp))
    exp_ids = [(p, lax.rem(e + k, n_exp)) for k in range(1, n_exp)]
    pos_ids = [(lax.rem(p + k, n_pos), e) for k in range(1, n_pos)]

    barrier = pltpu.get_barrier_semaphore()
    for device in [right_id, left_id] + exp_ids + pos_ids:
        pl.semaphore_signal(barrier, inc=1, device_id=device, device_id_type=MESH)

    def send(src, dst, s, r, device):
        copy = pltpu.make_async_remote_copy(
            src_ref=src, dst_ref=dst, send_sem=s, recv_sem=r,
            device_id=device, device_id_type=MESH,
        )
        copy.start()
        return copy

    x_copy = pltpu.make_async_copy(patches, x_raw, local_sem.at[0])
    x_copy.start()

    def tap_copy(n):
        cols = pl.ds(pl.multiple_of(n * chunk, chunk), chunk)
        return pltpu.make_async_copy(taps.at[:, cols], taps_v.at[:, cols], chunk_sem.at[n])

    for n in range(n_chunks):
        tap_copy(n).start()
    phi_copy = pltpu.make_async_copy(phi_t, phi_v, local_sem.at[1])
    phi_copy.start()

    x_copy.wait()
    x = x_raw[...].astype(F32).reshape(rows, samples)
    halo_out[0] = x[rows - 8 :]
    halo_out[1] = x[:8]
    xs[:, samples : 2 * samples] = x.astype(BF16)
    up = pltpu.roll(x, periods, 0)
    down = pltpu.roll(x, rows - periods, 0)
    xs[:, :samples] = up.astype(BF16)
    xs[:, 2 * samples :] = down.astype(BF16)

    pl.semaphore_wait(barrier, 2 + (n_exp - 1) + (n_pos - 1))
    halo = [
        send(halo_out.at[0], halo_in.at[0], halo_s.at[0], halo_r.at[0], right_id),
        send(halo_out.at[1], halo_in.at[1], halo_s.at[1], halo_r.at[1], left_id),
    ]

    def encode(n, begin, length):
        cols = pl.ds(pl.multiple_of(n * chunk, chunk), chunk)
        tokens[pl.ds(begin, length), cols] = jnp.dot(
            xs[pl.ds(begin, length), :], taps_v[:, cols], preferred_element_type=F32
        ).astype(BF16)

    @pl.loop(0, n_chunks)
    def _(n):
        tap_copy(n).wait()
        encode(n, edge, rows - 2 * edge)

    win_copy = pltpu.make_async_copy(w_in.at[0], win_v, local_sem.at[2])
    win_copy.start()
    wout_copy = pltpu.make_async_copy(w_out.at[0], wout_v, local_sem.at[3])
    wout_copy.start()

    for copy in halo:
        copy.wait()
    row16 = lax.broadcasted_iota(jnp.int32, (16, samples), 0)
    zero8 = jnp.zeros((8, samples), F32)
    before = jnp.concatenate([pltpu.roll(halo_in[0], 4, 0), zero8], axis=0)
    before = jnp.where(g == 0, 0.0, before)
    xs[0:16, :samples] = jnp.where(
        row16 < periods, before, xs[0:16, :samples].astype(F32)
    ).astype(BF16)
    after = jnp.concatenate([zero8, pltpu.roll(halo_in[1], 4, 0)], axis=0)
    after = jnp.where(g == count - 1, 0.0, after)
    xs[rows - 16 :, 2 * samples :] = jnp.where(
        row16 >= 16 - periods, after, xs[rows - 16 :, 2 * samples :].astype(F32)
    ).astype(BF16)

    @pl.loop(0, n_chunks)
    def _(n):
        encode(n, 0, edge)
        encode(n, rows - edge, edge)

    phi_copy.wait()
    contract_last = (((1,), (1,)), ((), ()))
    lg = lax.dot_general(tokens[...], phi_v[...], contract_last, preferred_element_type=F32)
    logits[...] = lg
    lt = lg.T
    peak = jnp.max(lt, axis=1, keepdims=True)
    weights = jnp.exp(lt - peak)
    total = jnp.sum(weights, axis=1, keepdims=True)
    lane = lax.broadcasted_iota(jnp.int32, (n_slots, 128), 1)
    stats = jnp.where(lane < 64, peak, total)
    for q in range(n_exp):
        stat_own[q] = stats[q * per : (q + 1) * per]
    stat_copies = [
        send(stat_own.at[ids[1]], stat_exp.at[k], stat_es.at[k], stat_er.at[k], ids)
        for k, ids in enumerate(exp_ids)
    ]
    sums = jnp.dot(weights.astype(BF16), tokens[...], preferred_element_type=F32)
    for q in range(n_exp):
        own = sums[q * per : (q + 1) * per]
        sum_own[q] = own
        sum_out[q] = pack(own)
    sum_copies = [
        send(sum_out.at[ids[1]], sum_exp.at[k], sum_s.at[k], sum_r.at[k], ids)
        for k, ids in enumerate(exp_ids)
    ]

    def merge(blocks):
        peaks = [b[:, 0:1] for b in blocks]
        totals = [b[:, 64:65] for b in blocks]
        top = functools.reduce(jnp.maximum, peaks)
        scales = [jnp.exp(v - top) for v in peaks]
        whole = functools.reduce(jnp.add, [s * t for s, t in zip(scales, totals)])
        return top, scales, whole

    for copy in stat_copies:
        copy.wait()
    top_e, scales_e, total_e = merge([stat_own[e]] + [stat_exp[k] for k in range(n_exp - 1)])
    lane8 = lax.broadcasted_iota(jnp.int32, (per, 128), 1)
    stat_mid[...] = jnp.where(lane8 < 64, top_e, total_e)
    stat_copies = [
        send(stat_mid, stat_pos.at[k], stat_ps.at[k], stat_pr.at[k], ids)
        for k, ids in enumerate(pos_ids)
    ]

    lg = logits[...]
    row_weights = jnp.exp(lg - jnp.max(lg, axis=1, keepdims=True))
    combine_ref[...] = (
        row_weights / jnp.sum(row_weights, axis=1, keepdims=True)
    ).astype(BF16)

    for copy in stat_copies:
        copy.wait()
    top, scales_p, total_all = merge([stat_mid[...]] + [stat_pos[k] for k in range(n_pos - 1)])
    factor = scales_p[0] / total_all

    for copy in sum_copies:
        copy.wait()
    part = scales_e[0] * sum_own[e]
    for k in range(n_exp - 1):
        part = part + scales_e[k + 1] * unpack(sum_exp[k], d)
    part = factor * part
    for q in range(n_pos):
        block = part[:, q * blk : (q + 1) * blk]
        part_own[q] = block
        part_out[q] = pack(block)
    part_copies = [
        send(part_out.at[ids[0]], part_pos.at[k], part_s.at[k], part_r.at[k], ids)
        for k, ids in enumerate(pos_ids)
    ]
    for copy in part_copies:
        copy.wait()
    mine = part_own[p]
    for k in range(n_pos - 1):
        mine = mine + unpack(part_pos[k], blk)
    in_own[...] = pack(mine)
    in_copies = [
        send(in_own, in_all.at[p], in_s.at[k], in_r.at[k], ids)
        for k, ids in enumerate(pos_ids)
    ]
    in_all[p] = in_own[...]
    win_copy.wait()
    for copy in in_copies:
        copy.wait()
    slot_in = jnp.concatenate(
        [unpack(in_all[q], blk) for q in range(n_pos)], axis=1
    ).astype(BF16)
    hidden = jax.nn.gelu(
        jnp.dot(slot_in, win_v[...], preferred_element_type=F32), approximate=True
    ).astype(BF16)
    wout_copy.wait()
    term = jnp.dot(hidden, wout_v[...], preferred_element_type=F32)
    for q in range(n_pos):
        block = term[:, q * blk : (q + 1) * blk]
        term_own[q] = block
        term_out[q] = pack(block)
    term_copies = [
        send(term_out.at[ids[0]], term_pos.at[k], term_s.at[k], term_r.at[k], ids)
        for k, ids in enumerate(pos_ids)
    ]
    for copy in term_copies:
        copy.wait()
    mine = term_own[p]
    for k in range(n_pos - 1):
        mine = mine + unpack(term_pos[k], blk)
    out_all[e, p] = pack(mine)
    slot_copies = [
        send(out_all.at[e, p], out_all.at[e, p], slot_s.at[k], slot_r.at[k], ids)
        for k, ids in enumerate(pos_ids)
    ]
    for copy in slot_copies:
        copy.wait()
    far_copies = [
        send(out_all.at[e], out_all.at[e], far_s.at[k], far_r.at[k], ids)
        for k, ids in enumerate(exp_ids)
    ]
    for copy in far_copies:
        copy.wait()
    slots_ref[...] = jnp.concatenate(
        [
            jnp.concatenate([unpack(out_all[i, q], blk) for q in range(n_pos)], axis=1)
            for i in range(n_exp)
        ],
        axis=0,
    ).astype(BF16)


def mix_kernel(combine_ref, slots_ref, out_ref):
    mixed = jnp.dot(combine_ref[...], slots_ref[...], preferred_element_type=F32)
    out_ref[...] = mixed.astype(BF16).reshape(out_ref.shape)


def per_device(n_pos, n_exp, patches, conv_weight, phi, w_in, w_out):
    channels, periods, samples = patches.shape
    rows = channels * periods
    d, n_slots = phi.shape
    ff = w_in.shape[2]
    per = n_slots // n_exp
    blk = d // n_pos
    chunk = 512
    wide, narrow = packed_shape(per, d), packed_shape(per, blk)
    dma = lambda *shape: pltpu.SemaphoreType.DMA(shape)
    any_spec = pl.BlockSpec(memory_space=pl.ANY)
    vmem_spec = pl.BlockSpec(memory_space=pltpu.VMEM)
    pairs = [2, 2, n_exp - 1, n_exp - 1, n_pos - 1, n_pos - 1, n_exp - 1, n_exp - 1]
    pairs += [n_pos - 1] * 8 + [n_exp - 1] * 2
    combine, slots = pl.pallas_call(
        functools.partial(layer_kernel, n_pos, n_exp, chunk),
        out_shape=(
            jax.ShapeDtypeStruct((rows, n_slots), BF16),
            jax.ShapeDtypeStruct((n_slots, d), BF16),
        ),
        in_specs=[any_spec] * 5,
        out_specs=(vmem_spec, vmem_spec),
        scratch_shapes=[
            pltpu.VMEM((channels, periods, samples), BF16),
            pltpu.VMEM((rows, 3 * samples), BF16),
            pltpu.VMEM((3 * samples, d), BF16),
            pltpu.VMEM((n_slots, d), BF16),
            pltpu.VMEM((d, ff), BF16),
            pltpu.VMEM((ff, d), BF16),
            pltpu.VMEM((rows, d), BF16),
            pltpu.VMEM((rows, n_slots), F32),
            pltpu.VMEM((2, 8, samples), F32),
            pltpu.VMEM((2, 8, samples), F32),
            pltpu.VMEM((n_exp, per, 128), F32),
            pltpu.VMEM((n_exp - 1, per, 128), F32),
            pltpu.VMEM((per, 128), F32),
            pltpu.VMEM((n_pos - 1, per, 128), F32),
            pltpu.VMEM((n_exp, per, d), F32),
            pltpu.VMEM((n_exp,) + wide, BF16),
            pltpu.VMEM((n_exp - 1,) + wide, BF16),
            pltpu.VMEM((n_pos, per, blk), F32),
            pltpu.VMEM((n_pos,) + narrow, BF16),
            pltpu.VMEM((n_pos - 1,) + narrow, BF16),
            pltpu.VMEM(narrow, BF16),
            pltpu.VMEM((n_pos,) + narrow, BF16),
            pltpu.VMEM((n_pos, per, blk), F32),
            pltpu.VMEM((n_pos,) + narrow, BF16),
            pltpu.VMEM((n_pos - 1,) + narrow, BF16),
            pltpu.VMEM((n_exp, n_pos) + narrow, BF16),
            dma(4),
            dma(d // chunk),
        ]
        + [dma(c) for c in pairs],
        compiler_params=pltpu.CompilerParams(
            collective_id=0, has_side_effects=True, vmem_limit_bytes=48 * 2**20
        ),
        name="moe_layer",
    )(patches, conv_weight.reshape(3 * samples, d), phi.T, w_in, w_out)
    step = 32
    return pl.pallas_call(
        mix_kernel,
        grid=(channels // step,),
        out_shape=jax.ShapeDtypeStruct((channels, periods, d), BF16),
        in_specs=[
            pl.BlockSpec((step * periods, n_slots), lambda i: (i, 0)),
            pl.BlockSpec((n_slots, d), lambda i: (0, 0)),
        ],
        out_specs=pl.BlockSpec((step, periods, d), lambda i: (i, 0, 0)),
        compiler_params=pltpu.CompilerParams(vmem_limit_bytes=32 * 2**20),
        name="mix_slots",
    )(combine, slots)


def solution(mesh):
    in_specs = (
        P(("pos", "exp"), None, None),
        P(),
        P(),
        P("exp", None, "pos"),
        P("exp", "pos", None),
    )
    out_specs = P(("pos", "exp"), None, None)
    body = functools.partial(per_device, mesh.shape["pos"], mesh.shape["exp"])
    return jax.shard_map(
        body, mesh=mesh, in_specs=in_specs, out_specs=out_specs, check_vma=False
    )
```

time: 224 us -> 51.3 us (0.23)
  blocking collectives: 169 us -> 0 us
  Pallas kernels: 0 us -> 47.2 us
  matrix products: 31.1 us -> 0 us
  local copies, waits for them, and re-layouts: 15.8 us -> 3.83 us
  starting transfers between devices: 3.64 us -> 0 us
  other arithmetic: 3.09 us -> 0 us
    psum x3 -> x0, blocking collectives: 119 us -> none  [the longest x1 42.5 us: per_device(): summed = lax.psum(every_slot, ('pos', 'exp'))]
    pallas_call x0 -> x2, Pallas kernels: none -> 47.2 us  [the longest x1 42.7 us: per_device(): pl.pallas_call(functools.partial(layer_kernel, n_pos, n_exp, chunk), out_...]
    pmax x1 -> x0, blocking collectives: 44.7 us -> none  [per_device(): column_peak = lax.pmax(local_peak, ('pos', 'exp'))]
    dot_general x7 -> x0, matrix products: 31.1 us -> none  [the longest x3 18.7 us: per_device(): jnp.dot(window, conv_weight[offset], preferred_element_type=jnp.float32)]
    reshape x4 -> x0, local copies, waits for them, and re-layouts: 13 us -> none  [the longest x1 7.16 us: per_device(): return mixed.astype(jnp.bfloat16).reshape(channels, periods, D)]
    all_gather x1 -> x0, blocking collectives: 5.42 us -> none  [per_device(): lax.all_gather(slot_out, 'exp', axis=0, tiled=True)]
    ppermute x2 -> x0, starting transfers between devices: 3.64 us -> none  [the longest x1 2.34 us: with_halo(): before = lax.ppermute(last, axis, up)]
    concatenate x1 -> x0, other arithmetic: 2.9 us -> none  [with_halo(): array = jnp.concatenate([before, array, after], axis=dim)]
  transfers between devices with their start and end apart: 2 -> 0, of which waited for: 0 -> 0; matrix products, arithmetic and copies ran while one was open for 4% -> 0% of each run, Pallas kernels for 0% -> 0%
where the time goes in v1:
time: 51.3 us; the launch traced here: 51.1 us
  Pallas kernels  47.2 us (92%)
  local copies, waits for them, and re-layouts  3.83 us (7%)
    pallas_call x1, Pallas kernels, per_device(): pl.pallas_call(functools.partial(layer_kernel, n_pos, n_exp, chunk), out_...  42.7 us
    pallas_call x1, Pallas kernels, per_device(): pl.pallas_call(mix_kernel, grid=(channels // step,), out_shape=jax.ShapeD...  4.57 us
    unnamed x6, local copies, waits for them, and re-layouts  3.83 us

profile of v1, /device:TPU:0, one launch (start us, length us, event | category | flops | bytes accessed | tf_op | source)
XLA Modules:
  0.0 51.1 jit_solution(3979417785838576041)
XLA Ops:
  0.0 0.0 copy-start
  0.0 1.9 %copy-done = bf16[3,256,2048]{2,1,0:T(8,128)(2,1)S(1)} copy-done((bf16[3,256,2048]{2,1,0:T(8,128)(2,1)S(1)}, bf16[3,256,2048]{2,1,0:T(8,128)(2,1)}, u32[]{:S(2)}) %copy-start) | copy-done | bytes 3145752
  1.9 0.0 copy-start.1
  1.9 1.0 %copy-done.1 = bf16[256,4,256]{2,1,0:T(4,128)(2,1)S(1)} copy-done((bf16[256,4,256]{2,1,0:T(4,128)(2,1)S(1)}, bf16[256,4,256]{2,1,0:T(4,128)(2,1)}, u32[]{:S(2)}) %copy-start.1) | copy-done | bytes 524312
  2.9 0.0 copy-start.2
  2.9 0.9 %copy-done.2 = bf16[2048,32]{0,1:T(8,128)(2,1)S(1)} copy-done((bf16[2048,32]{0,1:T(8,128)(2,1)S(1)}, bf16[2048,32]{0,1:T(8,128)(2,1)}, u32[]{:S(2)}) %copy-start.2) | copy-done | bytes 131096
  3.8 42.7 %moe_layer.1 = (bf16[1024,32]{1,0:T(8,128)(2,1)S(1)}, bf16[32,2048]{1,0:T(8,128)(2,1)S(1)}) custom-call(bf16[256,4,256]{2,1,0:T(4,128)(2,1)S(1)} %copy-done.1, bf16[768,2048]{1,0:T(8,128)(2,1)S(1)} %bitcast.2, bf16[32,2048]{1,0:T(8,128)(2,1)S(1)} %bitcast.3, bf16[1,2048,1024]{2,1,0:T(8,128)(2,1)} %w_in.1, bf16[1,1024,2048]{2,1,0:T(8,128)(2,1)} %w_out.1), custom_call_target="tpu_custom_call" | custom-call | tf_op jit(solution)/shard_map/moe_layer/pallas_call | solution.py:291
  46.5 4.6 %mix_slots.1 = bf16[256,4,2048]{2,1,0:T(4,128)(2,1)} custom-call(bf16[1024,32]{1,0:T(8,128)(2,1)S(1)} %get-tuple-element.7.combine_ref, bf16[32,2048]{1,0:T(8,128)(2,1)S(1)} %get-tuple-element.8.slots_ref), custom_call_target="tpu_custom_call" | custom-call | tf_op jit(solution)/shard_map/mix_slots/pallas_call | solution.py:336
Async XLA Ops:
  0.0 1.9 %copy-start = (bf16[3,256,2048]{2,1,0:T(8,128)(2,1)S(1)}, bf16[3,256,2048]{2,1,0:T(8,128)(2,1)}, u32[]{:S(2)}) copy-start(bf16[3,256,2048]{2,1,0:T(8,128)(2,1)} %param.6) | copy-start | bytes 9437188
  1.9 1.0 %copy-start.1 = (bf16[256,4,256]{2,1,0:T(4,128)(2,1)S(1)}, bf16[256,4,256]{2,1,0:T(4,128)(2,1)}, u32[]{:S(2)}) copy-start(bf16[256,4,256]{2,1,0:T(4,128)(2,1)} %patches.1) | copy-start | bytes 1572868
  2.9 0.9 %copy-start.2 = (bf16[2048,32]{0,1:T(8,128)(2,1)S(1)}, bf16[2048,32]{0,1:T(8,128)(2,1)}, u32[]{:S(2)}) copy-start(bf16[2048,32]{0,1:T(8,128)(2,1)} %param.7) | copy-start | bytes 393220

commit v2 on v1

v2 whole, which is shorter than its diff:
```python
import functools

import jax
import jax.numpy as jnp
from jax import lax
from jax.experimental import pallas as pl
from jax.experimental.pallas import tpu as pltpu
from jax.sharding import PartitionSpec as P

MESH = pl.DeviceIdType.MESH
F32 = jnp.float32
BF16 = jnp.bfloat16
FOLD = 2


def pack(block):
    rows, width = block.shape
    if width % 256 == 0:
        half = width // 2
        return jnp.concatenate([block[:, :half], block[:, half:]], axis=0).astype(BF16)
    return jnp.concatenate([block, jnp.zeros_like(block)], axis=0).astype(BF16)


def packed_shape(rows, width):
    return (2 * rows, width // 2 if width % 256 == 0 else width)


def unpack(block, width):
    wide = block.astype(F32)
    rows = wide.shape[0] // 2
    if width % 256 == 0:
        return jnp.concatenate([wide[:rows], wide[rows:]], axis=1)
    return wide[:rows]


def layer_kernel(
    n_pos, n_exp, chunk,
    patches, taps, phi_t, w_in, w_out,
    combine_ref, slots_ref,
    x_raw, xs, taps_v, phi_v, win_v, wout_v, tokens,
    halo_out, halo_in,
    stat_own, stat_plane, stat_z,
    sum_own, sum_out, sum_plane,
    in_all,
    term_out, term_pos,
    out_all, slots_v,
    local_sem, chunk_sem,
    halo_s, halo_r, stat_es, stat_er, stat_ps, stat_pr,
    sum_s, sum_r, in_s, in_r, term_s, term_r,
    slot_s, slot_r,
):
    p, e = lax.axis_index("pos"), lax.axis_index("exp")
    count = n_pos * n_exp
    g = p * n_exp + e
    channels, periods, samples = x_raw.shape
    rows = channels * periods
    d = tokens.shape[1]
    n_slots = phi_v.shape[0]
    per = n_slots // n_exp
    half = d // FOLD
    n_chunks = d // chunk
    edge = rows // 4

    right, left = lax.rem(g + 1, count), lax.rem(g + count - 1, count)
    right_id = (right // n_exp, lax.rem(right, n_exp))
    left_id = (left // n_exp, lax.rem(left, n_exp))
    z, x = p // FOLD, lax.rem(p, FOLD)
    n_z = n_pos // FOLD
    plane = [(a, b) for a in range(FOLD) for b in range(n_exp) if (a, b) != (0, 0)]
    plane_xe = [(lax.rem(x + a, FOLD), lax.rem(e + b, n_exp)) for a, b in plane]
    plane_ids = [(z * FOLD + a, b) for a, b in plane_xe]
    pos_p = [lax.rem(p + k, n_pos) for k in range(1, n_pos)]
    pos_ids = [(q, e) for q in pos_p]
    z_ids = [(lax.rem(z + k, n_z) * FOLD + x, e) for k in range(1, n_z)]

    barrier = pltpu.get_barrier_semaphore()
    for device in [right_id, left_id] + plane_ids + pos_ids:
        pl.semaphore_signal(barrier, inc=1, device_id=device, device_id_type=MESH)

    def send(src, dst, s, r, device):
        copy = pltpu.make_async_remote_copy(
            src_ref=src, dst_ref=dst, send_sem=s, recv_sem=r,
            device_id=device, device_id_type=MESH,
        )
        copy.start()
        return copy

    x_copy = pltpu.make_async_copy(patches, x_raw, local_sem.at[0])
    x_copy.start()

    def tap_copy(n):
        cols = pl.ds(pl.multiple_of(n * chunk, chunk), chunk)
        return pltpu.make_async_copy(taps.at[:, cols], taps_v.at[:, cols], chunk_sem.at[n])

    for n in range(n_chunks):
        tap_copy(n).start()
    phi_copy = pltpu.make_async_copy(phi_t, phi_v, local_sem.at[1])
    phi_copy.start()

    x_copy.wait()
    raw = x_raw[...].astype(F32).reshape(rows, samples)
    halo_out[0] = raw[rows - 8 :]
    halo_out[1] = raw[:8]
    xs[:, samples : 2 * samples] = raw.astype(BF16)
    up = pltpu.roll(raw, periods, 0)
    down = pltpu.roll(raw, rows - periods, 0)
    xs[:, :samples] = up.astype(BF16)
    xs[:, 2 * samples :] = down.astype(BF16)

    pl.semaphore_wait(barrier, 2 + len(plane_ids) + len(pos_ids))
    halo = [
        send(halo_out.at[0], halo_in.at[0], halo_s.at[0], halo_r.at[0], right_id),
        send(halo_out.at[1], halo_in.at[1], halo_s.at[1], halo_r.at[1], left_id),
    ]

    def encode(n, begin, length):
        cols = pl.ds(pl.multiple_of(n * chunk, chunk), chunk)
        tokens[pl.ds(begin, length), cols] = jnp.dot(
            xs[pl.ds(begin, length), :], taps_v[:, cols], preferred_element_type=F32
        ).astype(BF16)

    @pl.loop(0, n_chunks)
    def _(n):
        tap_copy(n).wait()
        encode(n, edge, rows - 2 * edge)

    win_copy = pltpu.make_async_copy(w_in.at[0], win_v, local_sem.at[2])
    win_copy.start()
    wout_copy = pltpu.make_async_copy(w_out.at[0], wout_v, local_sem.at[3])
    wout_copy.start()

    for copy in halo:
        copy.wait()
    row16 = lax.broadcasted_iota(jnp.int32, (16, samples), 0)
    zero8 = jnp.zeros((8, samples), F32)
    before = jnp.concatenate([pltpu.roll(halo_in[0], 4, 0), zero8], axis=0)
    before = jnp.where(g == 0, 0.0, before)
    xs[0:16, :samples] = jnp.where(
        row16 < periods, before, xs[0:16, :samples].astype(F32)
    ).astype(BF16)
    after = jnp.concatenate([zero8, pltpu.roll(halo_in[1], 4, 0)], axis=0)
    after = jnp.where(g == count - 1, 0.0, after)
    xs[rows - 16 :, 2 * samples :] = jnp.where(
        row16 >= 16 - periods, after, xs[rows - 16 :, 2 * samples :].astype(F32)
    ).astype(BF16)

    @pl.loop(0, n_chunks)
    def _(n):
        encode(n, 0, edge)
        encode(n, rows - edge, edge)

    phi_copy.wait()
    contract_last = (((1,), (1,)), ((), ()))
    lt = lax.dot_general(phi_v[...], tokens[...], contract_last, preferred_element_type=F32)
    peak = jnp.max(lt, axis=1, keepdims=True)
    weights = jnp.exp(lt - peak)
    total = jnp.sum(weights, axis=1, keepdims=True)
    lane = lax.broadcasted_iota(jnp.int32, (n_slots, 128), 1)
    stats = jnp.where(lane < 64, peak, total)
    for q in range(n_exp):
        stat_own[q] = stats[q * per : (q + 1) * per]
    stat_copies = [
        send(stat_own.at[to[1]], stat_plane.at[k], stat_es.at[k], stat_er.at[k], to)
        for k, to in enumerate(plane_ids)
    ]
    sums = jnp.dot(weights.astype(BF16), tokens[...], preferred_element_type=F32)
    for q in range(n_exp):
        for f in range(FOLD):
            own = sums[q * per : (q + 1) * per, f * half : (f + 1) * half]
            sum_own[f, q] = own
            sum_out[f, q] = pack(own)
    sum_copies = [
        send(sum_out.at[a, b], sum_plane.at[k], sum_s.at[k], sum_r.at[k], to)
        for k, ((a, b), to) in enumerate(zip(plane_xe, plane_ids))
    ]

    def merge(blocks):
        peaks = [b[:, 0:1] for b in blocks]
        totals = [b[:, 64:65] for b in blocks]
        top = functools.reduce(jnp.maximum, peaks)
        scales = [jnp.exp(v - top) for v in peaks]
        whole = functools.reduce(jnp.add, [s * t for s, t in zip(scales, totals)])
        return top, scales, whole

    for copy in stat_copies:
        copy.wait()
    top_p, scales_p, total_p = merge(
        [stat_own[e]] + [stat_plane[k] for k in range(len(plane_ids))]
    )
    lane8 = lax.broadcasted_iota(jnp.int32, (per, 128), 1)
    stat_z[z] = jnp.where(lane8 < 64, top_p, total_p)
    z_copies = [
        send(stat_z.at[z], stat_z.at[z], stat_ps.at[k], stat_pr.at[k], to)
        for k, to in enumerate(z_ids)
    ]

    row_weights = jnp.exp(lt - jnp.max(lt, axis=0, keepdims=True))
    combine = row_weights / jnp.sum(row_weights, axis=0, keepdims=True)
    combine_ref[...] = combine.T.astype(BF16)

    for copy in sum_copies:
        copy.wait()
    part = scales_p[0] * sum_own[x, e]
    for k in range(len(plane_ids)):
        part = part + scales_p[k + 1] * unpack(sum_plane[k], half)
    in_all[p] = pack(part)
    in_copies = [
        send(in_all.at[p], in_all.at[p], in_s.at[k], in_r.at[k], to)
        for k, to in enumerate(pos_ids)
    ]
    for copy in z_copies:
        copy.wait()
    top, scales_z, total_all = merge([stat_z[q] for q in range(n_z)])
    factors = [s / total_all for s in scales_z]
    win_copy.wait()
    for copy in in_copies:
        copy.wait()

    def gathered(f):
        terms = [factors[q] * unpack(in_all[q * FOLD + f], half) for q in range(n_z)]
        return functools.reduce(jnp.add, terms)

    slot_in = jnp.concatenate([gathered(f) for f in range(FOLD)], axis=1).astype(BF16)
    hidden = jax.nn.gelu(
        jnp.dot(slot_in, win_v[...], preferred_element_type=F32), approximate=True
    ).astype(BF16)
    wout_copy.wait()
    term = jnp.dot(hidden, wout_v[...], preferred_element_type=F32)
    for f in range(FOLD):
        term_out[f] = pack(term[:, f * half : (f + 1) * half])
    term_copies = [
        send(term_out.at[lax.rem(q, FOLD)], term_pos.at[p], term_s.at[k], term_r.at[k], to)
        for k, (q, to) in enumerate(zip(pos_p, pos_ids))
    ]
    term_pos[p] = term_out[x]
    for copy in term_copies:
        copy.wait()
    mine = functools.reduce(jnp.add, [unpack(term_pos[q], half) for q in range(n_pos)])
    out_all[e, x] = pack(mine)
    slot_copies = [
        send(out_all.at[e, x], out_all.at[e, x], slot_s.at[k], slot_r.at[k], to)
        for k, to in enumerate(plane_ids)
    ]
    for copy in slot_copies:
        copy.wait()
    for i in range(n_exp):
        for f in range(FOLD):
            slots_v[i * per : (i + 1) * per, f * half : (f + 1) * half] = unpack(
                out_all[i, f], half
            )
    slots_ref[...] = slots_v[...].astype(BF16)


def mix_kernel(combine_ref, slots_ref, out_ref):
    mixed = jnp.dot(combine_ref[...], slots_ref[...], preferred_element_type=F32)
    out_ref[...] = mixed.astype(BF16).reshape(out_ref.shape)


def per_device(n_pos, n_exp, patches, conv_weight, phi, w_in, w_out):
    channels, periods, samples = patches.shape
    rows = channels * periods
    d, n_slots = phi.shape
    ff = w_in.shape[2]
    per = n_slots // n_exp
    half = d // FOLD
    chunk = 512
    packed = packed_shape(per, half)
    n_plane = n_exp * FOLD - 1
    dma = lambda *shape: pltpu.SemaphoreType.DMA(shape)
    any_spec = pl.BlockSpec(memory_space=pltpu.HBM)
    vmem_spec = pl.BlockSpec(memory_space=pltpu.VMEM)
    pairs = [2, 2, n_plane, n_plane, n_pos // FOLD - 1, n_pos // FOLD - 1, n_plane, n_plane]
    pairs += [n_pos - 1] * 4 + [n_plane] * 2
    combine, slots = pl.pallas_call(
        functools.partial(layer_kernel, n_pos, n_exp, chunk),
        out_shape=(
            jax.ShapeDtypeStruct((rows, n_slots), BF16),
            jax.ShapeDtypeStruct((n_slots, d), BF16),
        ),
        in_specs=[any_spec] * 5,
        out_specs=(vmem_spec, vmem_spec),
        scratch_shapes=[
            pltpu.VMEM((channels, periods, samples), BF16),
            pltpu.VMEM((rows, 3 * samples), BF16),
            pltpu.VMEM((3 * samples, d), BF16),
            pltpu.VMEM((n_slots, d), BF16),
            pltpu.VMEM((d, ff), BF16),
            pltpu.VMEM((ff, d), BF16),
            pltpu.VMEM((rows, d), BF16),
            pltpu.VMEM((2, 8, samples), F32),
            pltpu.VMEM((2, 8, samples), F32),
            pltpu.VMEM((n_exp, per, 128), F32),
            pltpu.VMEM((n_plane, per, 128), F32),
            pltpu.VMEM((n_pos // FOLD, per, 128), F32),
            pltpu.VMEM((FOLD, n_exp, per, half), F32),
            pltpu.VMEM((FOLD, n_exp) + packed, BF16),
            pltpu.VMEM((n_plane,) + packed, BF16),
            pltpu.VMEM((n_pos,) + packed, BF16),
            pltpu.VMEM((FOLD,) + packed, BF16),
            pltpu.VMEM((n_pos,) + packed, BF16),
            pltpu.VMEM((n_exp, FOLD) + packed, BF16),
            pltpu.VMEM((n_slots, d), F32),
            dma(4),
            dma(d // chunk),
        ]
        + [dma(c) for c in pairs],
        compiler_params=pltpu.CompilerParams(
            collective_id=0, has_side_effects=True, vmem_limit_bytes=63 * 2**20
        ),
        name="moe_layer",
    )(patches, conv_weight.reshape(3 * samples, d), phi.T, w_in, w_out)
    step = 32
    return pl.pallas_call(
        mix_kernel,
        grid=(channels // step,),
        out_shape=jax.ShapeDtypeStruct((channels, periods, d), BF16),
        in_specs=[
            pl.BlockSpec((step * periods, n_slots), lambda i: (i, 0)),
            pl.BlockSpec((n_slots, d), lambda i: (0, 0)),
        ],
        out_specs=pl.BlockSpec((step, periods, d), lambda i: (i, 0, 0)),
        compiler_params=pltpu.CompilerParams(vmem_limit_bytes=63 * 2**20),
        name="mix_slots",
    )(combine, slots)


def solution(mesh):
    in_specs = (
        P(("pos", "exp"), None, None),
        P(),
        P(),
        P("exp", None, "pos"),
        P("exp", "pos", None),
    )
    out_specs = P(("pos", "exp"), None, None)
    body = functools.partial(per_device, mesh.shape["pos"], mesh.shape["exp"])
    return jax.shard_map(
        body, mesh=mesh, in_specs=in_specs, out_specs=out_specs, check_vma=False
    )
```

time: 51.3 us -> 40.4 us (0.79)
  Pallas kernels: 47.2 us -> 39.8 us
  local copies, waits for them, and re-layouts: 3.83 us -> 0 us
    pallas_call x1, Pallas kernels: 42.7 us -> 33.9 us  [per_device(): pl.pallas_call(functools.partial(layer_kernel, n_pos, n_exp, chunk), out_...]
    unnamed x6 -> x0, local copies, waits for them, and re-layouts: 3.83 us -> none
    pallas_call x1, Pallas kernels: 4.57 us -> 6 us  [per_device(): pl.pallas_call(mix_kernel, grid=(channels // step,), out_shape=jax.ShapeD...]
where the time goes in v2:
time: 40.4 us; the launch traced here: 39.9 us
  Pallas kernels  39.8 us (99%)
    pallas_call x1, Pallas kernels, per_device(): pl.pallas_call(functools.partial(layer_kernel, n_pos, n_exp, chunk), out_...  33.9 us
    pallas_call x1, Pallas kernels, per_device(): pl.pallas_call(mix_kernel, grid=(channels // step,), out_shape=jax.ShapeD...  6 us

profile of v2, /device:TPU:0, one launch (start us, length us, event | category | flops | bytes accessed | tf_op | source)
XLA Modules:
  0.0 39.9 jit_solution(7228422969005355891)
XLA Ops:
  0.0 33.9 %moe_layer.1 = (bf16[1024,32]{1,0:T(8,128)(2,1)}, bf16[32,2048]{1,0:T(8,128)(2,1)}) custom-call(bf16[256,4,256]{2,1,0:T(4,128)(2,1)} %patches.1, bf16[768,2048]{1,0:T(8,128)(2,1)} %bitcast.2, bf16[32,2048]{1,0:T(8,128)(2,1)} %bitcast.3, bf16[1,2048,1024]{2,1,0:T(8,128)(2,1)} %w_in.1, bf16[1,1024,2048]{2,1,0:T(8,128)(2,1)} %w_out.1), custom_call_target="tpu_custom_call" | custom-call | tf_op jit(solution)/shard_map/moe_layer/pallas_call | solution.py:274
  33.9 6.0 %mix_slots.1 = bf16[256,4,2048]{2,1,0:T(4,128)(2,1)} custom-call(bf16[1024,32]{1,0:T(8,128)(2,1)} %get-tuple-element.7.combine_ref, bf16[32,2048]{1,0:T(8,128)(2,1)} %get-tuple-element.8.slots_ref), custom_call_target="tpu_custom_call" | custom-call | tf_op jit(solution)/shard_map/mix_slots/pallas_call | solution.py:313

commit v3 on v2

--- a/solution.py
+++ b/solution.py
@@ -37,13 +37,13 @@
     n_pos, n_exp, chunk,
     patches, taps, phi_t, w_in, w_out,
     combine_ref, slots_ref,
-    x_raw, xs, taps_v, phi_v, win_v, wout_v, tokens,
+    x_raw, xs, xe, taps_v, phi_v, win_v, wout_v, tokens,
     halo_out, halo_in,
     stat_own, stat_plane, stat_z,
     sum_own, sum_out, sum_plane,
     in_all,
     term_out, term_pos,
-    out_all, slots_v,
+    out_all, slots_v, combine_v,
     local_sem, chunk_sem,
     halo_s, halo_r, stat_es, stat_er, stat_ps, stat_pr,
     sum_s, sum_r, in_s, in_r, term_s, term_r,
@@ -59,17 +59,22 @@
     per = n_slots // n_exp
     half = d // FOLD
     n_chunks = d // chunk
-    edge = rows // 4
+    edge = rows // 8
 
     right, left = lax.rem(g + 1, count), lax.rem(g + count - 1, count)
     right_id = (right // n_exp, lax.rem(right, n_exp))
     left_id = (left // n_exp, lax.rem(left, n_exp))
     z, x = p // FOLD, lax.rem(p, FOLD)
     n_z = n_pos // FOLD
-    plane = [(a, b) for a in range(FOLD) for b in range(n_exp) if (a, b) != (0, 0)]
+    plane = [(a, b) for a in reversed(range(FOLD)) for b in range(n_exp) if (a, b) != (0, 0)]
     plane_xe = [(lax.rem(x + a, FOLD), lax.rem(e + b, n_exp)) for a, b in plane]
     plane_ids = [(z * FOLD + a, b) for a, b in plane_xe]
-    pos_p = [lax.rem(p + k, n_pos) for k in range(1, n_pos)]
+    pos_p = [
+        lax.rem(z + k, n_z) * FOLD + lax.rem(x + a, FOLD)
+        for k in sorted(range(n_z), key=lambda k: k * (n_z - k) if k else n_z * n_z)
+        for a in reversed(range(FOLD))
+        if (k, a) != (0, 0)
+    ]
     pos_ids = [(q, e) for q in pos_p]
     z_ids = [(lax.rem(z + k, n_z) * FOLD + x, e) for k in range(1, n_z)]
 
@@ -113,16 +118,15 @@
         send(halo_out.at[1], halo_in.at[1], halo_s.at[1], halo_r.at[1], left_id),
     ]
 
-    def encode(n, begin, length):
+    def encode(n, source):
         cols = pl.ds(pl.multiple_of(n * chunk, chunk), chunk)
-        tokens[pl.ds(begin, length), cols] = jnp.dot(
-            xs[pl.ds(begin, length), :], taps_v[:, cols], preferred_element_type=F32
-        ).astype(BF16)
+        return cols, jnp.dot(source, taps_v[:, cols], preferred_element_type=F32).astype(BF16)
 
     @pl.loop(0, n_chunks)
     def _(n):
         tap_copy(n).wait()
-        encode(n, edge, rows - 2 * edge)
+        cols, value = encode(n, xs[edge : rows - edge])
+        tokens[edge : rows - edge, cols] = value
 
     win_copy = pltpu.make_async_copy(w_in.at[0], win_v, local_sem.at[2])
     win_copy.start()
@@ -144,10 +148,14 @@
         row16 >= 16 - periods, after, xs[rows - 16 :, 2 * samples :].astype(F32)
     ).astype(BF16)
 
+    xe[:edge] = xs[:edge]
+    xe[edge:] = xs[rows - edge :]
+
     @pl.loop(0, n_chunks)
     def _(n):
-        encode(n, 0, edge)
-        encode(n, rows - edge, edge)
+        cols, value = encode(n, xe[...])
+        tokens[:edge, cols] = value[:edge]
+        tokens[rows - edge :, cols] = value[edge:]
 
     phi_copy.wait()
     contract_last = (((1,), (1,)), ((), ()))
@@ -196,7 +204,9 @@
 
     row_weights = jnp.exp(lt - jnp.max(lt, axis=0, keepdims=True))
     combine = row_weights / jnp.sum(row_weights, axis=0, keepdims=True)
-    combine_ref[...] = combine.T.astype(BF16)
+    combine_v[...] = combine.T.astype(BF16)
+    combine_copy = pltpu.make_async_copy(combine_v, combine_ref, local_sem.at[4])
+    combine_copy.start()
 
     for copy in sum_copies:
         copy.wait()
@@ -241,6 +251,7 @@
         send(out_all.at[e, x], out_all.at[e, x], slot_s.at[k], slot_r.at[k], to)
         for k, to in enumerate(plane_ids)
     ]
+    combine_copy.wait()
     for copy in slot_copies:
         copy.wait()
     for i in range(n_exp):
@@ -251,9 +262,19 @@
     slots_ref[...] = slots_v[...].astype(BF16)
 
 
-def mix_kernel(combine_ref, slots_ref, out_ref):
-    mixed = jnp.dot(combine_ref[...], slots_ref[...], preferred_element_type=F32)
-    out_ref[...] = mixed.astype(BF16).reshape(out_ref.shape)
+def mix_kernel(step, combine_ref, slots_ref, out_ref, out_v, sem):
+    channels, periods, d = out_v.shape
+    copies = []
+    for i in range(channels // step):
+        part = pl.ds(i * step, step)
+        weights = combine_ref[i * step * periods : (i + 1) * step * periods]
+        mixed = jnp.dot(weights, slots_ref[...], preferred_element_type=F32)
+        out_v[part] = mixed.astype(BF16).reshape(step, periods, d)
+        copy = pltpu.make_async_copy(out_v.at[part], out_ref.at[part], sem.at[i])
+        copy.start()
+        copies.append(copy)
+    for copy in copies:
+        copy.wait()
 
 
 def per_device(n_pos, n_exp, patches, conv_weight, phi, w_in, w_out):
@@ -263,7 +284,7 @@
     ff = w_in.shape[2]
     per = n_slots // n_exp
     half = d // FOLD
-    chunk = 512
+    chunk = 1024
     packed = packed_shape(per, half)
     n_plane = n_exp * FOLD - 1
     dma = lambda *shape: pltpu.SemaphoreType.DMA(shape)
@@ -278,10 +299,11 @@
             jax.ShapeDtypeStruct((n_slots, d), BF16),
         ),
         in_specs=[any_spec] * 5,
-        out_specs=(vmem_spec, vmem_spec),
+        out_specs=(any_spec, vmem_spec),
         scratch_shapes=[
             pltpu.VMEM((channels, periods, samples), BF16),
             pltpu.VMEM((rows, 3 * samples), BF16),
+            pltpu.VMEM((rows // 4, 3 * samples), BF16),
             pltpu.VMEM((3 * samples, d), BF16),
             pltpu.VMEM((n_slots, d), BF16),
             pltpu.VMEM((d, ff), BF16),
@@ -300,7 +322,8 @@
             pltpu.VMEM((n_pos,) + packed, BF16),
             pltpu.VMEM((n_exp, FOLD) + packed, BF16),
             pltpu.VMEM((n_slots, d), F32),
-            dma(4),
+            pltpu.VMEM((rows, n_slots), BF16),
+            dma(5),
             dma(d // chunk),
         ]
         + [dma(c) for c in pairs],
@@ -311,14 +334,11 @@
     )(patches, conv_weight.reshape(3 * samples, d), phi.T, w_in, w_out)
     step = 32
     return pl.pallas_call(
-        mix_kernel,
-        grid=(channels // step,),
+        functools.partial(mix_kernel, step),
         out_shape=jax.ShapeDtypeStruct((channels, periods, d), BF16),
-        in_specs=[
-            pl.BlockSpec((step * periods, n_slots), lambda i: (i, 0)),
-            pl.BlockSpec((n_slots, d), lambda i: (0, 0)),
-        ],
-        out_specs=pl.BlockSpec((step, periods, d), lambda i: (i, 0, 0)),
+        in_specs=[vmem_spec, vmem_spec],
+        out_specs=any_spec,
+        scratch_shapes=[pltpu.VMEM((channels, periods, d), BF16), dma(channels // step)],
         compiler_params=pltpu.CompilerParams(vmem_limit_bytes=63 * 2**20),
         name="mix_slots",
     )(combine, slots)

time: 40.4 us -> 35.4 us (0.88)
  Pallas kernels: 39.8 us -> 35.2 us
    pallas_call x1, Pallas kernels: 6 us -> 3.32 us  [per_device(): pl.pallas_call(functools.partial(mix_kernel, step), out_shape=jax.ShapeDt...]
    pallas_call x1, Pallas kernels: 33.9 us -> 31.9 us  [per_device(): pl.pallas_call(functools.partial(layer_kernel, n_pos, n_exp, chunk), out_...]
where the time goes in v3:
time: 35.4 us; the launch traced here: 35.2 us
  Pallas kernels  35.2 us (99%)
    pallas_call x1, Pallas kernels, per_device(): pl.pallas_call(functools.partial(layer_kernel, n_pos, n_exp, chunk), out_...  31.9 us
    pallas_call x1, Pallas kernels, per_device(): pl.pallas_call(functools.partial(mix_kernel, step), out_shape=jax.ShapeDt...  3.32 us

profile of v3, /device:TPU:0, one launch (start us, length us, event | category | flops | bytes accessed | tf_op | source)
XLA Modules:
  0.0 35.2 jit_solution(13523811359161753847)
XLA Ops:
  0.0 31.9 %moe_layer.1 = (bf16[1024,32]{1,0:T(8,128)(2,1)}, bf16[32,2048]{1,0:T(8,128)(2,1)}) custom-call(bf16[256,4,256]{2,1,0:T(4,128)(2,1)} %patches.1, bf16[768,2048]{1,0:T(8,128)(2,1)} %bitcast.2, bf16[32,2048]{1,0:T(8,128)(2,1)} %bitcast.3, bf16[1,2048,1024]{2,1,0:T(8,128)(2,1)} %w_in.1, bf16[1,1024,2048]{2,1,0:T(8,128)(2,1)} %w_out.1), custom_call_target="tpu_custom_call" | custom-call | tf_op jit(solution)/shard_map/moe_layer/pallas_call | solution.py:295
  31.9 3.3 %mix_slots.1 = bf16[256,4,2048]{2,1,0:T(4,128)(2,1)} custom-call(bf16[1024,32]{1,0:T(8,128)(2,1)} %get-tuple-element.7.combine_ref, bf16[32,2048]{1,0:T(8,128)(2,1)} %get-tuple-element.8.slots_ref), custom_call_target="tpu_custom_call" | custom-call | tf_op jit(solution)/shard_map/mix_slots/pallas_call | solution.py:336
